TPU v7x, 512 devices: a whole 4x8x8 slice. The times are simulated.
512 devices in a mesh: rows: 128 (over z_hi, y, x), grp: 4 (over z_lo, core).
Axes of the slice: x: 4, y: 8, z: 8 (z_hi: 4, z_lo: 2; z = z_hi * 2 + z_lo), core: 2. Of those that a mesh axis runs over, the one named last changes fastest.
Arguments:
- features: bfloat16 [131072, 2048], P('rows', 'grp'), may hold values from -48 to 48
- clusters: int32 [131072], replicated, may hold values from 0 to 63, as said below
- bands: int32 [512], P('rows'), may hold values from 1 to 12, as said below
Outputs:
- max_cos: float32 [131072], P(('rows', 'grp'))
- dup_score: float32 [131072], P(('rows', 'grp'))
Inputs may be any that keep to these rules, and one draw needn't show every extreme that they name: `clusters`: ids never fall along the rows, start at 0 and rise by one where a new cluster begins. `bands`: some block has the width 12 in every draw.
All inputs are finite; a program needn't handle non-finite values.
Results may differ from a plain program's by a relative error of at most 0.0003.
Values may be sent and summed in bfloat16 or wider, within the bound.
A program may use at most 64 MiB of HBM per device.

v0:
```python
import jax
import jax.numpy as jnp
from jax import lax
from jax.sharding import PartitionSpec as P

BLOCK = 256
BAND = 12


SHARPNESS = 256.0
EPSILON = 1e-06


def shifted(block, axis, distance):
    devices = range(lax.axis_size(axis))
    route = [(i - distance, i) for i in devices if i - distance in devices]
    return lax.ppermute(block, axis, route)


def merged(part, axis, combine):
    gathered = jax.tree.map(lambda a: lax.all_gather(a, axis), part)

    def take(source):
        return jax.tree.map(lambda a: lax.dynamic_index_in_dim(a, source, 0, False), gathered)

    return lax.fori_loop(
        1, lax.axis_size(axis), lambda source, state: combine(state, take(source)), take(0)
    )


def merge_stats(former, latter):
    cos_former, sum_former = former
    cos_latter, sum_latter = latter
    cos_both = jnp.maximum(cos_former, cos_latter)
    base_both = jnp.maximum(0.0, SHARPNESS * cos_both)
    sum_both = sum_former * jnp.exp(
        jnp.maximum(0.0, SHARPNESS * cos_former) - base_both
    ) + sum_latter * jnp.exp(jnp.maximum(0.0, SHARPNESS * cos_latter) - base_both)
    return (cos_both, sum_both)


def masked_stats(cosine, chosen, axis):
    top_cos = jnp.max(jnp.where(chosen, cosine, -1.0), axis=axis)
    base_exp = jnp.maximum(0.0, SHARPNESS * top_cos)
    exponent = jnp.where(chosen, SHARPNESS * cosine - jnp.expand_dims(base_exp, axis), -10000.0)
    return (top_cos, jnp.sum(jnp.exp(exponent), axis=axis))


def finish(top_cos, summed):
    base_exp = jnp.maximum(0.0, SHARPNESS * top_cos)
    return base_exp + jnp.log(jnp.exp(-base_exp) + summed)


def inverse_norms(values):
    return lax.rsqrt(jnp.sum(jnp.square(values.astype(jnp.float32)), axis=1) + EPSILON)


def on_device(features, clusters, bands):
    rows_dev = features.shape[0]
    groups = lax.axis_size("grp")
    row_count = lax.axis_size("rows")
    position = lax.axis_index("rows")
    member = lax.axis_index("grp")
    quarter = rows_dev // groups
    blocks_dev = rows_dev // BLOCK
    reach_dev = (BAND + blocks_dev - 1) // blocks_dev
    own_full = lax.all_gather(features, "grp", axis=1, tiled=True)
    query_inv = inverse_norms(own_full)
    query_rows = position * rows_dev + jnp.arange(rows_dev, dtype=jnp.int32)
    query_block = query_rows // BLOCK
    local_block = jnp.arange(rows_dev, dtype=jnp.int32) // BLOCK
    query_band = jnp.sum(
        jnp.where(
            local_block[:, None] == jnp.arange(blocks_dev, dtype=jnp.int32)[None, :],
            bands[None, :],
            0,
        ),
        axis=1,
    )
    query_reach = query_block + query_band
    query_cluster = lax.dynamic_slice_in_dim(clusters, position * rows_dev, rows_dev)
    own_keys = lax.dynamic_slice_in_dim(own_full, member * quarter, quarter, 0)
    row_stats = (jnp.full((rows_dev,), -1.0, jnp.float32), jnp.zeros((rows_dev,), jnp.float32))
    returned = []
    current = own_keys
    for offset in range(reach_dev + 1):
        if offset > 0:
            current = shifted(own_keys, "rows", -offset)
        first_row = (position + offset) * rows_dev + member * quarter
        key_rows = first_row + jnp.arange(quarter, dtype=jnp.int32)
        key_block = key_rows // BLOCK
        key_cluster = lax.dynamic_slice_in_dim(
            clusters, jnp.minimum(first_row, clusters.shape[0] - quarter), quarter
        )
        in_range = position + offset < row_count
        same_group = (query_cluster[:, None] == key_cluster[None, :]) & in_range
        forward = (key_block[None, :] > query_block[:, None]) & (
            key_block[None, :] <= query_reach[:, None]
        )
        same_block = (key_block[None, :] == query_block[:, None]) & (
            key_rows[None, :] != query_rows[:, None]
        )
        products = lax.dot_general(
            own_full, current, (((1,), (1,)), ((), ())), preferred_element_type=jnp.float32
        )
        cosine = products * query_inv[:, None] * inverse_norms(current)[None, :]
        row_top, row_sum = masked_stats(cosine, same_group & (forward | same_block), 1)
        col_top, col_sum = masked_stats(cosine, same_group & forward, 0)
        row_top, row_sum, col_top, col_sum = (row_top, row_sum, col_top, col_sum)
        row_stats = merge_stats(row_stats, (row_top, row_sum))
        returned.append((col_top, col_sum))
    merged_top, merged_sum = merged((row_stats[0], row_stats[1]), "grp", merge_stats)
    own_part = (
        lax.dynamic_slice_in_dim(merged_top, member * quarter, quarter),
        lax.dynamic_slice_in_dim(merged_sum, member * quarter, quarter),
    )
    mirrored = returned[0]
    for offset in range(1, reach_dev + 1):
        moved_top, moved_sum = shifted((returned[offset][0], returned[offset][1]), "rows", offset)
        moved = (
            jnp.where(position >= offset, moved_top, -1.0),
            jnp.where(position >= offset, moved_sum, 0.0),
        )
        mirrored = merge_stats(mirrored, moved)
    max_cos, summed = merge_stats(own_part, mirrored)
    return (max_cos, finish(max_cos, summed))


def solution(mesh):
    placed = (P("rows", "grp"), P(), P("rows"))
    return jax.shard_map(
        on_device,
        mesh=mesh,
        in_specs=placed,
        out_specs=(P(("rows", "grp")), P(("rows", "grp"))),
        check_vma=False,
    )
```

profile of v0, /device:TPU:108, one launch (start us, length us, event | category | flops | bytes accessed | tf_op | source)
XLA Modules:
  0.0 254.9 jit_solution(4721279623051995363)
XLA Ops:
  7.2 0.0 all-gather.4.cloned.1.call-start
  7.2 0.7 all-gather.4.cloned.1.call-update
  8.0 0.9 fusion.27
  8.9 0.7 select_reduce_fusion.8
  9.6 54.2 %all-gather.4.cloned.1.call-done = bf16[1024,2048]{1,0:T(8,128)(2,1)} async-done(((bf16[1024,512]{1,0:T(8,128)(2,1)}), bf16[1024,2048]{1,0:T(8,128)(2,1)}) %all-gather.4.cloned.1.call-update) | async-done | bytes 4194320 | tf_op jit(solution)/shard_map/all_gather | solution.py:67
  63.8 1.5 multiply_reduce_fusion.4
  65.3 4.0 %collective-permute-start.2 = (bf16[256,2048]{1,0:T(8,128)(2,1)S(1)}, bf16[256,2048]{1,0:T(8,128)(2,1)S(1)}, u32[]{:S(2)}, u32[]{:S(2)}) collective-permute-start(bf16[256,2048]{1,0:T(8,128)(2,1)S(1)} %get-tuple-element.178), channel_id=1, source_target_pairs={{12,0},{16,4},{20,8},{24,12},{28,16},{32,20},{36,24},{40,28},{44,3... | collective-permute-start | bytes 3145736 | tf_op jit(solution)/shard_map/ppermute | solution.py:17
  69.3 0.0 copy-start
  69.3 0.8 dynamic_slice.51
  70.2 2.9 %collective-permute-start.1 = (bf16[256,2048]{1,0:T(8,128)(2,1)S(1)}, bf16[256,2048]{1,0:T(8,128)(2,1)S(1)}, u32[]{:S(2)}, u32[]{:S(2)}) collective-permute-start(bf16[256,2048]{1,0:T(8,128)(2,1)S(1)} %get-tuple-element.178), channel_id=1, source_target_pairs={{8,0},{12,4},{16,8},{20,12},{24,16},{28,20},{32,24},{36,28},{40,32... | collective-permute-start | bytes 3145736 | tf_op jit(solution)/shard_map/ppermute | solution.py:17
  73.1 3.1 %collective-permute-start = (bf16[256,2048]{1,0:T(8,128)(2,1)S(1)}, bf16[256,2048]{1,0:T(8,128)(2,1)S(1)}, u32[]{:S(2)}, u32[]{:S(2)}) collective-permute-start(bf16[256,2048]{1,0:T(8,128)(2,1)S(1)} %get-tuple-element.178), channel_id=1, source_target_pairs={{4,0},{8,4},{12,8},{16,12},{20,16},{24,20},{28,24},{32,28},{36,32}... | collective-permute-start | bytes 3145736 | tf_op jit(solution)/shard_map/ppermute | solution.py:17
  76.2 3.1 %multiply_reduce_fusion = f32[1024]{0:T(1024)S(1)} fusion(bf16[1024,2048]{1,0:T(8,128)(2,1)} %all-gather.4.cloned.1.call-done), kind=kLoop, calls=%fused_computation.3 | loop fusion | flops 6290432 | bytes 4198400 | tf_op jit(solution)/shard_map/reduce_sum | solution.py:55
  79.3 14.9 %collective-permute-done.2 = bf16[256,2048]{1,0:T(8,128)(2,1)S(1)} collective-permute-done((bf16[256,2048]{1,0:T(8,128)(2,1)S(1)}, bf16[256,2048]{1,0:T(8,128)(2,1)S(1)}, u32[]{:S(2)}, u32[]{:S(2)}) %collective-permute-start.2) | collective-permute-done | bytes 1048608 | tf_op jit(solution)/shard_map/ppermute | solution.py:17
  94.2 0.3 multiply_reduce_fusion.1
  94.4 0.0 copy-done
  94.5 1.9 select_reduce_fusion.4
  96.4 2.6 %select_reduce_fusion.7 = (f32[1024]{0:T(1024)S(1)}, f32[256]{0:T(256)S(1)}, f32[1024]{0:T(1024)S(1)}, f32[256]{0:T(256)S(1)}, f32[1024,256]{0,1:T(8,128)S(1)}) fusion(s32[1024]{0:T(1024)S(1)} %iota_add_fusion, s32[256]{0:T(256)S(1)} %get-tuple-element.194, s32[1024]{0:T(1024)S(1)} %get-tuple-element.192, s32[1024]{0:T(1024)S(1)} %get-tuple-element.191, ...), kind=kOutput, calls=%fused_computation.35 | convolution fusion | flops 1082914304 | bytes 7383042 | tf_op jit(solution)/shard_map/dot_general | solution.py:103
  99.0 17.6 %collective-permute-done.1 = bf16[256,2048]{1,0:T(8,128)(2,1)S(1)} collective-permute-done((bf16[256,2048]{1,0:T(8,128)(2,1)S(1)}, bf16[256,2048]{1,0:T(8,128)(2,1)S(1)}, u32[]{:S(2)}, u32[]{:S(2)}) %collective-permute-start.1) | collective-permute-done | bytes 1048608 | tf_op jit(solution)/shard_map/ppermute | solution.py:17
  116.6 0.3 multiply_reduce_fusion.2
  116.9 2.6 %select_reduce_fusion.5 = (f32[1024]{0:T(1024)S(1)}, f32[256]{0:T(256)S(1)}, f32[1024]{0:T(1024)S(1)}, f32[256]{0:T(256)S(1)}, f32[1024,256]{0,1:T(8,128)S(1)}) fusion(s32[1024]{0:T(1024)S(1)} %iota_add_fusion, s32[256]{0:T(256)S(1)} %get-tuple-element.196, s32[1024]{0:T(1024)S(1)} %get-tuple-element.192, s32[1024]{0:T(1024)S(1)} %get-tuple-element.191, ...), kind=kOutput, calls=%fused_computation.33 | convolution fusion | flops 1082914304 | bytes 7383042 | tf_op jit(solution)/shard_map/dot_general | solution.py:103
  119.5 1.7 collective-permute-done
  121.2 0.3 multiply_reduce_fusion.3
  121.5 2.6 %select_reduce_fusion.6 = (f32[1024]{0:T(1024)S(1)}, f32[256]{0:T(256)S(1)}, f32[1024]{0:T(1024)S(1)}, f32[256]{0:T(256)S(1)}, f32[1024,256]{0,1:T(8,128)S(1)}) fusion(s32[1024]{0:T(1024)S(1)} %iota_add_fusion, s32[256]{0:T(256)S(1)} %get-tuple-element.198, s32[1024]{0:T(1024)S(1)} %get-tuple-element.192, s32[1024]{0:T(1024)S(1)} %get-tuple-element.191, ...), kind=kOutput, calls=%fused_computation.34 | convolution fusion | flops 1082914304 | bytes 7383042 | tf_op jit(solution)/shard_map/dot_general | solution.py:103
  124.1 1.1 exponential_reduce_fusion.2
  125.2 5.2 %all-gather = f32[4096]{0:T(1024)S(1)} all-gather(f32[1024]{0:T(1024)S(1)} %get-tuple-element.176), channel_id=2, replica_groups=mesh['rows'=128,'grp'=4] {'grp'}, dimensions={0}, use_global_device_ids=true | all-gather | bytes 20480 | tf_op jit(solution)/shard_map/all_gather | solution.py:21
  130.4 21.8 %collective-permute-start.6 = (f32[256]{0:T(256)S(1)}, f32[256]{0:T(256)S(1)}, u32[]{:S(2)}, u32[]{:S(2)}) collective-permute-start(f32[256]{0:T(256)S(1)} %get-tuple-element.139), channel_id=1, source_target_pairs={{0,4},{4,8},{8,12},{12,16},{16,20},{20,24},{24,28},{28,32},{32,36}... | collective-permute-start | bytes 3080 | tf_op jit(solution)/shard_map/ppermute | solution.py:17
  152.2 5.2 %all-gather.1 = f32[4,1,1024]{2,1,0:T(1,128)S(1)} all-gather(f32[1,1,1024]{2,1,0:T(1,128)S(1)} %add_bitcast_fusion), channel_id=1, replica_groups=mesh['rows'=128,'grp'=4] {'grp'}, dimensions={0}, use_global_device_ids=true | all-gather | bytes 20480 | tf_op jit(solution)/shard_map/all_gather | solution.py:21
  157.4 1.9 collective-permute-start.3
  159.4 1.9 collective-permute-start.4
  161.3 3.9 %collective-permute-start.5 = (f32[256]{0:T(256)S(1)}, f32[256]{0:T(256)S(1)}, u32[]{:S(2)}, u32[]{:S(2)}) collective-permute-start(f32[256]{0:T(256)S(1)} %get-tuple-element.146), channel_id=1, source_target_pairs={{0,12},{4,16},{8,20},{12,24},{16,28},{20,32},{24,36},{28,40},{32,4... | collective-permute-start | bytes 3080 | tf_op jit(solution)/shard_map/ppermute | solution.py:17
  165.3 75.8 %collective-permute-start.7 = (f32[256]{0:T(256)S(1)}, f32[256]{0:T(256)S(1)}, u32[]{:S(2)}, u32[]{:S(2)}) collective-permute-start(f32[256]{0:T(256)S(1)} %get-tuple-element.156), channel_id=1, source_target_pairs={{0,8},{4,12},{8,16},{12,20},{16,24},{20,28},{24,32},{28,36},{32,40... | collective-permute-start | bytes 3080 | tf_op jit(solution)/shard_map/ppermute | solution.py:17
  241.1 0.0 collective-permute-done.6
  241.1 1.9 collective-permute-start.8
  243.0 0.2 while.17
  243.2 0.0 collective-permute-done.3
  243.2 0.0 collective-permute-done.7
  243.2 0.0 collective-permute-done.4
  243.2 4.2 %collective-permute-done.8 = f32[256]{0:T(256)S(1)} collective-permute-done((f32[256]{0:T(256)S(1)}, f32[256]{0:T(256)S(1)}, u32[]{:S(2)}, u32[]{:S(2)}) %collective-permute-start.8) | collective-permute-done | bytes 1056 | tf_op jit(solution)/shard_map/ppermute | solution.py:17
  247.4 0.0 collective-permute-done.5
  247.4 0.7 log_add_fusion
  (34 shorter events, 0.3 us)
Async XLA Ops:
  7.2 56.6 %all-gather.4.cloned.1.call-start = ((), (), s32[]{:S(2)}) async-start(), calls=%async_computation | async-start | bytes 5242880 | tf_op jit(solution)/shard_map/all_gather | solution.py:67
  65.3 28.8 %collective-permute-start.2 = (bf16[256,2048]{1,0:T(8,128)(2,1)S(1)}, bf16[256,2048]{1,0:T(8,128)(2,1)S(1)}, u32[]{:S(2)}, u32[]{:S(2)}) collective-permute-start(bf16[256,2048]{1,0:T(8,128)(2,1)S(1)} %get-tuple-element.178), channel_id=1, source_target_pairs={{12,0},{16,4},{20,8},{24,12},{28,16},{32,20},{36,24},{40,28},{44,3... | collective-permute-start | bytes 3145736 | tf_op jit(solution)/shard_map/ppermute | solution.py:17
  69.3 25.1 %copy-start = (bf16[1024,2048]{1,0:T(8,128)(2,1)S(1)}, bf16[1024,2048]{1,0:T(8,128)(2,1)}, u32[]{:S(2)}) copy-start(bf16[1024,2048]{1,0:T(8,128)(2,1)} %all-gather.4.cloned.1.call-done) | copy-start | bytes 12582916
  70.2 46.4 %collective-permute-start.1 = (bf16[256,2048]{1,0:T(8,128)(2,1)S(1)}, bf16[256,2048]{1,0:T(8,128)(2,1)S(1)}, u32[]{:S(2)}, u32[]{:S(2)}) collective-permute-start(bf16[256,2048]{1,0:T(8,128)(2,1)S(1)} %get-tuple-element.178), channel_id=1, source_target_pairs={{8,0},{12,4},{16,8},{20,12},{24,16},{28,20},{32,24},{36,28},{40,32... | collective-permute-start | bytes 3145736 | tf_op jit(solution)/shard_map/ppermute | solution.py:17
  73.1 48.1 %collective-permute-start = (bf16[256,2048]{1,0:T(8,128)(2,1)S(1)}, bf16[256,2048]{1,0:T(8,128)(2,1)S(1)}, u32[]{:S(2)}, u32[]{:S(2)}) collective-permute-start(bf16[256,2048]{1,0:T(8,128)(2,1)S(1)} %get-tuple-element.178), channel_id=1, source_target_pairs={{4,0},{8,4},{12,8},{16,12},{20,16},{24,20},{28,24},{32,28},{36,32}... | collective-permute-start | bytes 3145736 | tf_op jit(solution)/shard_map/ppermute | solution.py:17
  130.4 110.6 %collective-permute-start.6 = (f32[256]{0:T(256)S(1)}, f32[256]{0:T(256)S(1)}, u32[]{:S(2)}, u32[]{:S(2)}) collective-permute-start(f32[256]{0:T(256)S(1)} %get-tuple-element.139), channel_id=1, source_target_pairs={{0,4},{4,8},{8,12},{12,16},{16,20},{20,24},{24,28},{28,32},{32,36}... | collective-permute-start | bytes 3080 | tf_op jit(solution)/shard_map/ppermute | solution.py:17
  157.4 85.7 %collective-permute-start.3 = (f32[256]{0:T(256)S(1)}, f32[256]{0:T(256)S(1)}, u32[]{:S(2)}, u32[]{:S(2)}) collective-permute-start(f32[256]{0:T(256)S(1)} %get-tuple-element.150), channel_id=1, source_target_pairs={{0,4},{4,8},{8,12},{12,16},{16,20},{20,24},{24,28},{28,32},{32,36}... | collective-permute-start | bytes 3080 | tf_op jit(solution)/shard_map/ppermute | solution.py:17
  159.4 83.8 %collective-permute-start.4 = (f32[256]{0:T(256)S(1)}, f32[256]{0:T(256)S(1)}, u32[]{:S(2)}, u32[]{:S(2)}) collective-permute-start(f32[256]{0:T(256)S(1)} %get-tuple-element.152), channel_id=1, source_target_pairs={{0,8},{4,12},{8,16},{12,20},{16,24},{20,28},{24,32},{28,36},{32,40... | collective-permute-start | bytes 3080 | tf_op jit(solution)/shard_map/ppermute | solution.py:17
  161.3 86.1 %collective-permute-start.5 = (f32[256]{0:T(256)S(1)}, f32[256]{0:T(256)S(1)}, u32[]{:S(2)}, u32[]{:S(2)}) collective-permute-start(f32[256]{0:T(256)S(1)} %get-tuple-element.146), channel_id=1, source_target_pairs={{0,12},{4,16},{8,20},{12,24},{16,28},{20,32},{24,36},{28,40},{32,4... | collective-permute-start | bytes 3080 | tf_op jit(solution)/shard_map/ppermute | solution.py:17
  165.3 77.9 %collective-permute-start.7 = (f32[256]{0:T(256)S(1)}, f32[256]{0:T(256)S(1)}, u32[]{:S(2)}, u32[]{:S(2)}) collective-permute-start(f32[256]{0:T(256)S(1)} %get-tuple-element.156), channel_id=1, source_target_pairs={{0,8},{4,12},{8,16},{12,20},{16,24},{20,28},{24,32},{28,36},{32,40... | collective-permute-start | bytes 3080 | tf_op jit(solution)/shard_map/ppermute | solution.py:17
  241.1 6.4 %collective-permute-start.8 = (f32[256]{0:T(256)S(1)}, f32[256]{0:T(256)S(1)}, u32[]{:S(2)}, u32[]{:S(2)}) collective-permute-start(f32[256]{0:T(256)S(1)} %get-tuple-element.158), channel_id=1, source_target_pairs={{0,12},{4,16},{8,20},{12,24},{16,28},{20,32},{24,36},{28,40},{32,4... | collective-permute-start | bytes 3080 | tf_op jit(solution)/shard_map/ppermute | solution.py:17
Sparse Core Ops, SparseCore 0:
  10.1 53.6 all-gather.3
where the time goes:
time: 256 us; the launch traced here: 255 us
  starting transfers between devices  117 us (46%)
  waiting for transfers between devices  93.3 us (36%)
  between operations  14.3 us (6%)
  blocking collectives  10.4 us (4%)
  matrix products  9.63 us (4%)
  other arithmetic  8.16 us (3%)
    ppermute x9, starting transfers between devices, shifted(): return lax.ppermute(block, axis, route)  117 us
    all_gather x1, waiting for transfers between devices, on_device(): own_full = lax.all_gather(features, 'grp', axis=1, tiled=True)  54.2 us
    ppermute x9, waiting for transfers between devices, shifted(): return lax.ppermute(block, axis, route)  38.5 us
    all_gather x2, blocking collectives, merged(): gathered = jax.tree.map(lambda a: lax.all_gather(a, axis), part)  10.4 us
    dot_general x4, matrix products, on_device(): lax.dot_general(own_full, current, (((1,), (1,)), ((), ())), preferred_el...  9.63 us
    reduce_sum x5, other arithmetic, inverse_norms(): jnp.sum(jnp.square(values.astype(jnp.float32)), axis=1) + EPSILON  5.44 us
  transfers between devices with their start and end apart: 10, of which 5 were waited for; matrix products, arithmetic and copies ran while one was open for 5% of the time, Pallas kernels for 0%

commit v1 on v0

v1 whole, which is shorter than its diff:
```python
import functools
import math

import jax
import jax.numpy as jnp
from jax import lax
from jax.experimental import pallas as pl
from jax.experimental.pallas import tpu as pltpu
from jax.sharding import PartitionSpec as P

MESH = pl.DeviceIdType.MESH
BLOCK = 256
SHARPNESS = 256.0
EPSILON = 1e-06
SCALE = SHARPNESS * math.log2(math.e)
MASKED = -1e30

NEXT1, NEXT2, NEXT3, PASS1, PASS2 = range(5)
ORDER = (0, 1, 3, 2)


def as_row(column):
    return jnp.transpose(jnp.broadcast_to(column, (column.shape[0], 128)))[0:1, :]


def as_column(row):
    return jnp.transpose(jnp.broadcast_to(row, (128, row.shape[1])))[:, 0:1]


def merge(former, latter):
    top = jnp.maximum(former[0], latter[0])
    base = jnp.maximum(0.0, top)
    summed = former[1] * jnp.exp2(jnp.maximum(0.0, former[0]) - base) + latter[1] * jnp.exp2(
        jnp.maximum(0.0, latter[0]) - base
    )
    return (top, summed)


def kernel(
    runs,
    features,
    clusters,
    bands,
    top_out,
    score_out,
    whole,
    ahead,
    work,
    labels,
    key_msg,
    key_got,
    query_msg,
    query_got,
    load_sem,
    label_sem,
    whole_send,
    whole_recv,
    pass_send,
    ahead_send,
    ahead_recv,
    key_send,
    key_recv,
    query_send,
    query_recv,
):
    p = lax.axis_index("rows")
    m = lax.axis_index("grp")
    core = m % 2
    column = p % 4
    ring = p - column

    def at(run, member):
        return {"rows": run, "grp": member}

    def mate(j):
        low = (m + j) % 2
        high = (m // 2 + j // 2) % 2
        return high * 2 + low

    def shifted(distance):
        return (p + distance + runs) % runs

    left = ring + (column + 3) % 4
    right = ring + (column + 1) % 4
    below = shifted(-4)
    above = shifted(4)

    loads = []
    for j in range(4):
        start = pl.multiple_of(mate(j) * BLOCK, BLOCK)
        loads.append(
            pltpu.make_async_copy(features.at[pl.ds(start, BLOCK)], whole.at[0, j], load_sem.at[j])
        )
    for j in (1, 3, 2, 0):
        loads[j].start()
    label_loads = []
    for i in range(4):
        start = pl.multiple_of(shifted(i) * 8, 8)
        label_loads.append(
            pltpu.make_async_copy(clusters.at[pl.ds(start, 8)], labels.at[i], label_sem.at[i])
        )
        label_loads[i].start()

    barrier = pltpu.get_barrier_semaphore()
    greeted = [at(p, mate(j)) for j in (1, 2, 3)]
    greeted += [at(run, m) for run in (left, right, above, shifted(-1), shifted(-2), shifted(-3))]
    for device in greeted:
        pl.semaphore_signal(barrier, inc=1, device_id=device, device_id_type=MESH)
    for j in range(4):
        loads[j].wait()
    pl.semaphore_wait(barrier, len(greeted))

    def group_copy(piece, j, to_piece, to_j, partner, send_sem):
        return pltpu.make_async_remote_copy(
            src_ref=whole.at[piece, j],
            dst_ref=whole.at[to_piece, to_j],
            send_sem=send_sem,
            recv_sem=whole_recv.at[to_piece, to_j],
            device_id=at(p, mate(partner)),
            device_id_type=MESH,
        )

    def to_core(j):
        return group_copy(0, j, 1, j ^ 1, 1, whole_send.at[0, j])

    def to_chip(j):
        return group_copy(0, j, 2, j ^ 2, 2, whole_send.at[1, j])

    def pass_on(j):
        return group_copy(2, j, 3, j ^ 1, 1, pass_send.at[j])

    def arrived(piece, j):
        group_copy(0, j, piece, j, 1, whole_send.at[0, 0]).wait_recv()

    def ahead_copy(kind, source, r, run, slot):
        return pltpu.make_async_remote_copy(
            src_ref=source,
            dst_ref=ahead.at[slot, r],
            send_sem=ahead_send.at[kind, r],
            recv_sem=ahead_recv.at[slot, r],
            device_id=at(run, m),
            device_id_type=MESH,
        )

    def ahead_arrived(slot, r):
        ahead_copy(0, whole.at[0, 0], r, p, slot).wait_recv()

    even, odd = core == 0, core == 1

    def send_own(r):
        own = whole.at[r, 0]

        @pl.when(column != 0)
        def _():
            ahead_copy(0, own, r, left, NEXT1).start()

        @pl.when((even & (column == 3)) | (odd & (column >= 2)))
        def _():
            slot = jnp.where(odd & (column == 2), PASS1, NEXT3)
            ahead_copy(2, own, r, right, slot).start()

        @pl.when((even & (column < 3)) | (odd & (column < 2)))
        def _():
            ahead_copy(3, own, r, below, PASS1).start()

    def relay_pass(r):
        passing = ahead.at[PASS1, r]

        @pl.when((even & (column < 3)) | (odd & (column != 2)))
        def _():
            ahead_arrived(PASS1, r)

        @pl.when(column == 0)
        def _():
            ahead_copy(0, passing, r, left, NEXT1).start()

        @pl.when((even & (column < 3)) | (odd & (column < 2)))
        def _():
            ahead_copy(2, passing, r, right, NEXT3).start()

        @pl.when(odd & (column == 3))
        def _():
            ahead_copy(3, passing, r, below, NEXT3).start()
            ahead_copy(1, passing, r, right, NEXT2).start()

    def relay_next(r):
        @pl.when(even)
        def _():
            ahead_arrived(NEXT1, r)

            @pl.when(column == 0)
            def _():
                ahead_copy(4, ahead.at[NEXT1, r], r, below, PASS2).start()

            @pl.when(column != 0)
            def _():
                ahead_copy(1, ahead.at[NEXT1, r], r, left, NEXT2).start()

        @pl.when(odd & (column < 3))
        def _():
            ahead_arrived(NEXT3, r)
            ahead_copy(1, ahead.at[NEXT3, r], r, right, NEXT2).start()

    def relay_second(r):
        @pl.when(even & (column == 0))
        def _():
            ahead_arrived(PASS2, r)
            ahead_copy(1, ahead.at[PASS2, r], r, left, NEXT2).start()

    to_core(1).start()
    to_chip(3).start()
    to_chip(2).start()
    send_own(0)
    for j in (0, 2, 3):
        to_core(j).start()
    arrived(1, 0)
    send_own(1)
    relay_pass(0)
    arrived(2, 1)
    pass_on(1).start()
    arrived(3, 0)
    send_own(3)
    relay_pass(1)
    arrived(2, 0)
    send_own(2)
    pass_on(0).start()
    to_chip(3).wait_send()
    to_chip(2).wait_send()
    to_chip(1).start()
    to_chip(0).start()
    relay_pass(3)
    relay_next(0)
    relay_pass(2)
    relay_next(1)
    arrived(2, 2)
    pass_on(2).start()
    relay_next(3)
    arrived(2, 3)
    pass_on(3).start()
    relay_next(2)
    for r in ORDER:
        relay_second(r)

    for j in (1, 2, 3):
        arrived(1, j)
    for j in (1, 2, 3):
        arrived(3, j)
    for i in range(4):
        label_loads[i].wait()

    def inverse_norm(blocks):
        squares = [jnp.square(b.astype(jnp.float32)) for b in blocks]
        return lax.rsqrt(
            jnp.sum(squares[0] + squares[1] + squares[2] + squares[3], axis=1, keepdims=True)
            + EPSILON
        )

    def label_row(i, block):
        return jnp.concatenate(
            [labels[i, pl.ds(2 * block, 1), :], labels[i, pl.ds(2 * block + 1, 1), :]], axis=1
        )

    query_inv, query_label = [], []
    own_inv = None
    for j in range(4):
        inv = inverse_norm([whole[r, j] for r in range(4)])
        own_inv = inv if j == 0 else own_inv
        query_inv.append(as_row(inv))
        query_label.append(label_row(0, mate(j)))

    def tile(i, keys, inv):
        label = as_column(label_row(i, m).astype(jnp.float32)).astype(jnp.int32)
        label = jnp.where(p + i < runs, label, -2)
        key_scale = inv * SCALE
        key_top = jnp.full((BLOCK, 1), MASKED, jnp.float32)
        key_sum = jnp.zeros((BLOCK, 1), jnp.float32)
        tops = []
        for j in range(4):
            products = None
            for r in range(4):
                term = lax.dot_general(
                    keys[r], whole[r, j], (((1,), (1,)), ((), ())), preferred_element_type=jnp.float32
                )
                products = term if products is None else products + term
            block = mate(j)
            if i > 0:
                valid = 4 * i + m - block <= bands[block]
            elif j > 0:
                valid = jnp.where(block > m, block - m <= bands[m], m - block <= bands[block])
            else:
                valid = True
            query = query_label[j] if valid is True else jnp.where(valid, query_label[j], -1)
            chosen = label == query
            if i == 0 and j == 0:
                rows = lax.broadcasted_iota(jnp.int32, (BLOCK, BLOCK), 0)
                columns = lax.broadcasted_iota(jnp.int32, (BLOCK, BLOCK), 1)
                chosen = chosen & (rows != columns)
            scaled = jnp.where(chosen, products * key_scale * query_inv[j], MASKED)
            work[:, j * BLOCK : (j + 1) * BLOCK] = scaled
            key_top = jnp.maximum(key_top, jnp.max(scaled, axis=1, keepdims=True))
            if i > 0:
                tops.append(jnp.max(scaled, axis=0, keepdims=True))
        key_base = jnp.maximum(0.0, key_top)
        sums = []
        for j in range(4):
            scaled = work[:, j * BLOCK : (j + 1) * BLOCK]
            key_sum += jnp.sum(jnp.exp2(scaled - key_base), axis=1, keepdims=True)
            if i > 0:
                base = jnp.maximum(0.0, tops[j])
                sums.append(jnp.sum(jnp.exp2(scaled - base), axis=0, keepdims=True))
        return (as_row(key_top), as_row(key_sum)), list(zip(tops, sums))

    own, _ = tile(0, [whole[r, 0] for r in range(4)], own_inv)

    def key_copy(i):
        return pltpu.make_async_remote_copy(
            src_ref=key_msg.at[i - 1],
            dst_ref=key_got.at[i - 1],
            send_sem=key_send.at[i - 1],
            recv_sem=key_recv.at[i - 1],
            device_id=at(shifted(i), m),
            device_id_type=MESH,
        )

    def query_copy(j):
        return pltpu.make_async_remote_copy(
            src_ref=query_msg.at[j - 1],
            dst_ref=query_got.at[j - 1],
            send_sem=query_send.at[j - 1],
            recv_sem=query_recv.at[j - 1],
            device_id=at(p, mate(j)),
            device_id_type=MESH,
        )

    running = None
    for i, slot in ((1, NEXT1), (3, NEXT3), (2, NEXT2)):
        for r in ORDER:
            if slot == NEXT1:
                @pl.when(odd)
                def _():
                    ahead_arrived(NEXT1, r)
            elif slot == NEXT3:
                @pl.when(even | (column == 3))
                def _():
                    ahead_arrived(NEXT3, r)
            else:
                ahead_arrived(NEXT2, r)
        keys = [ahead[slot, r] for r in range(4)]
        key_stats, query_stats = tile(i, keys, inverse_norm(keys))
        key_msg[i - 1, 0:1, :] = key_stats[0]
        key_msg[i - 1, 1:2, :] = key_stats[1]
        key_copy(i).start()
        if running is None:
            running = query_stats
        else:
            running = [merge(a, b) for a, b in zip(running, query_stats)]

    for j in (3, 2, 1):
        query_msg[j - 1, 0:1, :] = running[j][0]
        query_msg[j - 1, 1:2, :] = running[j][1]
        query_copy(j).start()
    state = merge(own, running[0])

    for r in range(4):
        ahead_copy(0, whole.at[0, 0], r, p, NEXT1).wait_send()
        ahead_copy(1, whole.at[0, 0], r, p, NEXT1).wait_send()
        ahead_copy(2, whole.at[0, 0], r, p, NEXT1).wait_send()

        @pl.when((even & (column < 3)) | (odd & (column != 2)))
        def _():
            ahead_copy(3, whole.at[0, 0], r, p, NEXT1).wait_send()

        @pl.when(even & (column == 0))
        def _():
            ahead_copy(4, whole.at[0, 0], r, p, NEXT1).wait_send()

    for j in range(4):
        to_core(j).wait_send()
        pass_on(j).wait_send()
    to_chip(1).wait_send()
    to_chip(0).wait_send()
    for i in (1, 3, 2):
        key_copy(i).wait()
        state = merge(state, (key_got[i - 1, 0:1, :], key_got[i - 1, 1:2, :]))
    for j in (1, 2, 3):
        query_copy(j).wait()
        state = merge(state, (query_got[j - 1, 0:1, :], query_got[j - 1, 1:2, :]))
    top, summed = state
    base = jnp.maximum(0.0, top)
    top_out[...] = jnp.maximum(-1.0, top * (1.0 / SCALE))
    score_out[...] = base * math.log(2.0) + jnp.log(jnp.exp2(-base) + summed)


def on_device(features, clusters, bands):
    runs = lax.axis_size("rows")
    rows, width = features.shape
    dma = pltpu.SemaphoreType.DMA
    top, score = pl.pallas_call(
        functools.partial(kernel, runs),
        out_shape=[jax.ShapeDtypeStruct((1, BLOCK), jnp.float32)] * 2,
        in_specs=[
            pl.BlockSpec(memory_space=pl.ANY),
            pl.BlockSpec(memory_space=pl.ANY),
            pl.BlockSpec(memory_space=pltpu.SMEM),
        ],
        out_specs=[pl.BlockSpec(memory_space=pltpu.VMEM)] * 2,
        scratch_shapes=[
            pltpu.VMEM((4, 4, BLOCK, width), jnp.bfloat16),
            pltpu.VMEM((5, 4, BLOCK, width), jnp.bfloat16),
            pltpu.VMEM((BLOCK, rows), jnp.float32),
            pltpu.VMEM((4, 8, 128), jnp.int32),
            pltpu.VMEM((3, 8, BLOCK), jnp.float32),
            pltpu.VMEM((3, 8, BLOCK), jnp.float32),
            pltpu.VMEM((3, 8, BLOCK), jnp.float32),
            pltpu.VMEM((3, 8, BLOCK), jnp.float32),
            dma((4,)),
            dma((4,)),
            dma((2, 4)),
            dma((4, 4)),
            dma((4,)),
            dma((5, 4)),
            dma((5, 4)),
            dma((3,)),
            dma((3,)),
            dma((3,)),
            dma((3,)),
        ],
        compiler_params=pltpu.CompilerParams(
            collective_id=0, has_side_effects=True, vmem_limit_bytes=48 * 1024 * 1024
        ),
        name="screen",
    )(features, clusters.reshape(-1, 128), bands)
    return (top.reshape(-1), score.reshape(-1))


def solution(mesh):
    placed = (P("rows", "grp"), P(), P("rows"))
    return jax.shard_map(
        on_device,
        mesh=mesh,
        in_specs=placed,
        out_specs=(P(("rows", "grp")), P(("rows", "grp"))),
        check_vma=False,
    )
```

time: 256 us -> 133 us (0.52)
  the two profiles are of different devices: /device:TPU:108 before, /device:TPU:2 now
where the time goes in v1:
time: 133 us
  Pallas kernels  128 us (96%)
  local copies, waits for them, and re-layouts  4.04 us (3%)
    pallas_call x1, Pallas kernels, on_device(): pl.pallas_call(functools.partial(kernel, runs), out_shape=[jax.ShapeDtype...  128 us
    unnamed x8, local copies, waits for them, and re-layouts  4.04 us

profile of v1, /device:TPU:2, one launch (start us, length us, event | category | flops | bytes accessed | tf_op | source)
XLA Modules:
  0.0 132.6 jit_solution(11606797043866240245)
XLA Ops:
  0.6 0.0 copy-start.2
  0.6 0.6 copy-done.2
  1.3 0.0 copy-start
  1.3 1.2 copy-done
  2.5 0.0 copy-start.1
  2.5 1.0 copy-done.1
  3.6 127.9 %screen.1 = (f32[1,256]{1,0:T(1,128)S(1)}, f32[1,256]{1,0:T(1,128)S(1)}) custom-call(bf16[1024,512]{1,0:T(8,128)(2,1)S(1)} %copy-done, s32[1024,128]{1,0:T(8,128)S(1)} %bitcast.3, s32[4]{0:T(128)S(1)} %copy-done.2), custom_call_target="tpu_custom_call" | custom-call | tf_op jit(solution)/shard_map/screen/pallas_call | solution.py:398
  131.5 0.6 copy.7
  132.0 0.6 copy.8
Async XLA Ops:
  0.6 0.7 copy-start.2
  1.3 1.2 copy-start
  2.5 1.0 copy-start.1

commit v2 on v1

--- a/solution.py
+++ b/solution.py
@@ -15,7 +15,9 @@
 SCALE = SHARPNESS * math.log2(math.e)
 MASKED = -1e30
 
-NEXT1, NEXT2, NEXT3, PASS1, PASS2 = range(5)
+NEXT1, NEXT2, NEXT3, PASS1, PASS2, VIA1, VIA2 = range(7)
+Z_FIRST = (0, 3)
+FIRST = 0
 ORDER = (0, 1, 3, 2)
 
 
@@ -40,7 +42,7 @@
     runs,
     features,
     clusters,
-    bands,
+    bands_in,
     top_out,
     score_out,
     whole,
@@ -51,6 +53,7 @@
     key_got,
     query_msg,
     query_got,
+    bands,
     load_sem,
     label_sem,
     whole_send,
@@ -84,6 +87,10 @@
     right = ring + (column + 1) % 4
     below = shifted(-4)
     above = shifted(4)
+    layer = 32
+    first_ring = (p // 4) % 8 == 0
+    last_ring = (p // 4) % 8 == 7
+    near, far = m // 2 == 0, m // 2 == 1
 
     loads = []
     for j in range(4):
@@ -101,14 +108,38 @@
         )
         label_loads[i].start()
 
+    label_loads.append(pltpu.make_async_copy(bands_in, bands, label_sem.at[4]))
+    label_loads[4].start()
+
     barrier = pltpu.get_barrier_semaphore()
     greeted = [at(p, mate(j)) for j in (1, 2, 3)]
     greeted += [at(run, m) for run in (left, right, above, shifted(-1), shifted(-2), shifted(-3))]
     for device in greeted:
         pl.semaphore_signal(barrier, inc=1, device_id=device, device_id_type=MESH)
+
+    def greet(run, member):
+        pl.semaphore_signal(barrier, inc=1, device_id=at(run, member), device_id_type=MESH)
+
+    @pl.when(first_ring)
+    def _():
+        greet(shifted(layer), m)
+
+        @pl.when(far)
+        def _():
+            greet(shifted(layer), mate(2))
+
+    @pl.when(last_ring)
+    def _():
+        greet(shifted(4 - layer), m)
+
+        @pl.when(far)
+        def _():
+            greet(above, mate(2))
+
     for j in range(4):
         loads[j].wait()
-    pl.semaphore_wait(barrier, len(greeted))
+    extra = jnp.where(first_ring, jnp.where(near, 4, 2), 0)
+    pl.semaphore_wait(barrier, len(greeted) + extra)
 
     def group_copy(piece, j, to_piece, to_j, partner, send_sem):
         return pltpu.make_async_remote_copy(
@@ -132,13 +163,13 @@
     def arrived(piece, j):
         group_copy(0, j, piece, j, 1, whole_send.at[0, 0]).wait_recv()
 
-    def ahead_copy(kind, source, r, run, slot):
+    def ahead_copy(kind, source, r, run, slot, member=m):
         return pltpu.make_async_remote_copy(
             src_ref=source,
             dst_ref=ahead.at[slot, r],
             send_sem=ahead_send.at[kind, r],
             recv_sem=ahead_recv.at[slot, r],
-            device_id=at(run, m),
+            device_id=at(run, member),
             device_id_type=MESH,
         )
 
@@ -146,6 +177,13 @@
         ahead_copy(0, whole.at[0, 0], r, p, slot).wait_recv()
 
     even, odd = core == 0, core == 1
+    drops = (even & (column < 3)) | (odd & (column < 2))
+
+    def send_below(kind, source, r, slot, ring_kind):
+        if ring_kind == FIRST and r in Z_FIRST:
+            ahead_copy(kind, source, r, shifted(-layer), VIA1).start()
+        else:
+            ahead_copy(kind, source, r, below, slot).start()
 
     def send_own(r):
         own = whole.at[r, 0]
@@ -159,68 +197,140 @@
             slot = jnp.where(odd & (column == 2), PASS1, NEXT3)
             ahead_copy(2, own, r, right, slot).start()
 
-        @pl.when((even & (column < 3)) | (odd & (column < 2)))
-        def _():
-            ahead_copy(3, own, r, below, PASS1).start()
+        @pl.when(drops & ~first_ring)
+        def _():
+            send_below(3, own, r, PASS1, None)
+
+        @pl.when(drops & first_ring & near)
+        def _():
+            send_below(3, own, r, PASS1, FIRST)
+
+    def send_other(piece):
+        r = piece ^ 2
+
+        @pl.when(drops & first_ring & near)
+        def _():
+            if piece in (1, 3):
+                arrived(piece, 2)
+            run, slot = (shifted(-layer), VIA1) if r in Z_FIRST else (below, PASS1)
+            ahead_copy(7, whole.at[piece, 2], r, run, slot, mate(2)).start()
+
+    def relay_layer(r):
+        @pl.when(drops)
+        def _():
+            ahead_arrived(VIA1, r)
+            ahead_copy(5, ahead.at[VIA1, r], r, shifted(layer - 4), PASS1).start()
+
+    def relay_layer_late(r):
+        @pl.when(odd & (column == 3))
+        def _():
+            ahead_arrived(VIA1, r)
+            ahead_copy(5, ahead.at[VIA1, r], r, shifted(layer - 4), NEXT3).start()
 
     def relay_pass(r):
         passing = ahead.at[PASS1, r]
 
-        @pl.when((even & (column < 3)) | (odd & (column != 2)))
+        @pl.when(drops)
         def _():
             ahead_arrived(PASS1, r)
+            ahead_copy(2, passing, r, right, NEXT3).start()
 
         @pl.when(column == 0)
         def _():
             ahead_copy(0, passing, r, left, NEXT1).start()
 
-        @pl.when((even & (column < 3)) | (odd & (column < 2)))
-        def _():
-            ahead_copy(2, passing, r, right, NEXT3).start()
+    def relay_cross(r, ring_kind):
+        passing = ahead.at[PASS1, r]
 
         @pl.when(odd & (column == 3))
         def _():
-            ahead_copy(3, passing, r, below, NEXT3).start()
+            ahead_arrived(PASS1, r)
+            send_below(3, passing, r, NEXT3, ring_kind)
             ahead_copy(1, passing, r, right, NEXT2).start()
 
-    def relay_next(r):
-        @pl.when(even)
+    def relay_soon(r, ring_kind):
+        @pl.when(even & (column < 3))
         def _():
             ahead_arrived(NEXT1, r)
 
-            @pl.when(column == 0)
-            def _():
-                ahead_copy(4, ahead.at[NEXT1, r], r, below, PASS2).start()
+            if ring_kind != FIRST:
+                @pl.when(column == 0)
+                def _():
+                    ahead_copy(4, ahead.at[NEXT1, r], r, below, PASS2).start()
 
             @pl.when(column != 0)
             def _():
                 ahead_copy(1, ahead.at[NEXT1, r], r, left, NEXT2).start()
 
-        @pl.when(odd & (column < 3))
+        @pl.when(odd & (column == 0))
         def _():
             ahead_arrived(NEXT3, r)
             ahead_copy(1, ahead.at[NEXT3, r], r, right, NEXT2).start()
 
+    def relay_later(r):
+        @pl.when(even & (column == 3))
+        def _():
+            ahead_arrived(NEXT1, r)
+            ahead_copy(1, ahead.at[NEXT1, r], r, left, NEXT2).start()
+
+        @pl.when(odd & ((column == 1) | (column == 2)))
+        def _():
+            ahead_arrived(NEXT3, r)
+            ahead_copy(1, ahead.at[NEXT3, r], r, right, NEXT2).start()
+
+    def relay_last(r):
+        @pl.when(even & (column == 2))
+        def _():
+            ahead_arrived(NEXT3, r)
+            ahead_copy(4, ahead.at[NEXT3, r], r, right, NEXT2).start()
+
     def relay_second(r):
         @pl.when(even & (column == 0))
         def _():
             ahead_arrived(PASS2, r)
             ahead_copy(1, ahead.at[PASS2, r], r, left, NEXT2).start()
+
+    def relay_rest(piece):
+        arrived(2, piece)
+        pass_on(piece).start()
 
     to_core(1).start()
     to_chip(3).start()
     to_chip(2).start()
     send_own(0)
-    for j in (0, 2, 3):
+    for j in (2, 0, 3):
         to_core(j).start()
+    send_other(0)
     arrived(1, 0)
     send_own(1)
-    relay_pass(0)
+    send_other(1)
+
+    @pl.when(~last_ring)
+    def _():
+        relay_pass(0)
+
+    @pl.when(first_ring)
+    def _():
+        relay_layer(jnp.where(far, 3, 0))
+
+    @pl.when(last_ring)
+    def _():
+        relay_soon(0, None)
+        relay_cross(0, None)
+
     arrived(2, 1)
     pass_on(1).start()
     arrived(3, 0)
     send_own(3)
-    relay_pass(1)
+
+    @pl.when(~last_ring)
+    def _():
+        relay_pass(1)
+
+    @pl.when(last_ring)
+    def _():
+        relay_pass(jnp.where(far, 2, 1))
+
     arrived(2, 0)
     send_own(2)
     pass_on(0).start()
@@ -228,24 +338,87 @@
     to_chip(2).wait_send()
     to_chip(1).start()
     to_chip(0).start()
-    relay_pass(3)
-    relay_next(0)
-    relay_pass(2)
-    relay_next(1)
-    arrived(2, 2)
-    pass_on(2).start()
-    relay_next(3)
-    arrived(2, 3)
-    pass_on(3).start()
-    relay_next(2)
-    for r in ORDER:
-        relay_second(r)
-
-    for j in (1, 2, 3):
+
+    @pl.when(~first_ring & ~last_ring)
+    def _():
+        for r, then in ((3, 0), (2, 1)):
+            relay_pass(r)
+            relay_cross(then, None)
+            relay_soon(then, None)
+            relay_later(then)
+        relay_rest(2)
+        relay_cross(3, None)
+        relay_soon(3, None)
+        relay_later(3)
+        relay_rest(3)
+        relay_cross(2, None)
+        relay_soon(2, None)
+        relay_later(2)
+        for r in ORDER:
+            relay_second(r)
+
+    @pl.when(first_ring)
+    def _():
+        relay_soon(0, FIRST)
+
+        @pl.when(near)
+        def _():
+            relay_layer(3)
+
+        relay_pass(3)
+        relay_rest(2)
+        send_other(2)
+        relay_soon(1, FIRST)
+        relay_rest(3)
+        send_other(3)
+        relay_pass(2)
+
+        @pl.when(far)
+        def _():
+            relay_layer(0)
+
+        relay_cross(0, FIRST)
+        relay_cross(1, FIRST)
+        for r in (3, 2):
+            relay_soon(r, FIRST)
+            relay_cross(r, FIRST)
+        for r in ORDER:
+            relay_later(r)
+        relay_layer_late(0)
+        relay_layer_late(3)
+        for r in ORDER:
+            relay_second(r)
+
+    @pl.when(last_ring)
+    def _():
+        coming = [jnp.where(far, a, b) for a, b in zip((2, 3, 1, 0), (1, 0, 2, 3))]
+        relay_soon(1, None)
+        relay_cross(1, None)
+        relay_pass(coming[1])
+        relay_rest(2)
+        relay_soon(3, None)
+        relay_cross(3, None)
+        relay_rest(3)
+        relay_soon(2, None)
+        relay_cross(2, None)
+        relay_pass(coming[2])
+        relay_later(coming[0])
+        relay_pass(coming[3])
+        for r in coming[1:]:
+            relay_later(r)
+        for r in coming:
+            relay_last(r)
+
+    for j in (1, 3):
         arrived(1, j)
-    for j in (1, 2, 3):
         arrived(3, j)
-    for i in range(4):
+
+    @pl.when(~(drops & first_ring & near))
+    def _():
+        arrived(1, 2)
+        arrived(3, 2)
+
+    for i in range(5):
         label_loads[i].wait()
 
     def inverse_norm(blocks):
@@ -340,7 +513,7 @@
                 def _():
                     ahead_arrived(NEXT1, r)
             elif slot == NEXT3:
-                @pl.when(even | (column == 3))
+                @pl.when((even & ~((column == 2) & last_ring)) | (odd & (column == 3)))
                 def _():
                     ahead_arrived(NEXT3, r)
             else:
@@ -361,18 +534,33 @@
         query_copy(j).start()
     state = merge(own, running[0])
 
+    def sent(kind, r):
+        ahead_copy(kind, whole.at[0, 0], r, p, NEXT1).wait_send()
+
     for r in range(4):
-        ahead_copy(0, whole.at[0, 0], r, p, NEXT1).wait_send()
-        ahead_copy(1, whole.at[0, 0], r, p, NEXT1).wait_send()
-        ahead_copy(2, whole.at[0, 0], r, p, NEXT1).wait_send()
-
-        @pl.when((even & (column < 3)) | (odd & (column != 2)))
-        def _():
-            ahead_copy(3, whole.at[0, 0], r, p, NEXT1).wait_send()
-
-        @pl.when(even & (column == 0))
-        def _():
-            ahead_copy(4, whole.at[0, 0], r, p, NEXT1).wait_send()
+        sent(0, r)
+        sent(2, r)
+
+        @pl.when(~(last_ring & even & (column == 0)))
+        def _():
+            sent(1, r)
+
+        @pl.when((drops & ~(first_ring & far)) | (odd & (column == 3)))
+        def _():
+            sent(3, r)
+
+        @pl.when(drops & first_ring & near)
+        def _():
+            sent(7, r)
+
+        @pl.when(even & (((column == 0) & ~first_ring) | ((column == 2) & last_ring)))
+        def _():
+            sent(4, r)
+
+        if r in Z_FIRST:
+            @pl.when(first_ring & (drops | (odd & (column == 3))))
+            def _():
+                sent(5, r)
 
     for j in range(4):
         to_core(j).wait_send()
@@ -399,34 +587,35 @@
         functools.partial(kernel, runs),
         out_shape=[jax.ShapeDtypeStruct((1, BLOCK), jnp.float32)] * 2,
         in_specs=[
-            pl.BlockSpec(memory_space=pl.ANY),
-            pl.BlockSpec(memory_space=pl.ANY),
-            pl.BlockSpec(memory_space=pltpu.SMEM),
+            pl.BlockSpec(memory_space=pltpu.HBM),
+            pl.BlockSpec(memory_space=pltpu.HBM),
+            pl.BlockSpec(memory_space=pltpu.HBM),
         ],
         out_specs=[pl.BlockSpec(memory_space=pltpu.VMEM)] * 2,
         scratch_shapes=[
             pltpu.VMEM((4, 4, BLOCK, width), jnp.bfloat16),
-            pltpu.VMEM((5, 4, BLOCK, width), jnp.bfloat16),
+            pltpu.VMEM((7, 4, BLOCK, width), jnp.bfloat16),
             pltpu.VMEM((BLOCK, rows), jnp.float32),
             pltpu.VMEM((4, 8, 128), jnp.int32),
             pltpu.VMEM((3, 8, BLOCK), jnp.float32),
             pltpu.VMEM((3, 8, BLOCK), jnp.float32),
             pltpu.VMEM((3, 8, BLOCK), jnp.float32),
             pltpu.VMEM((3, 8, BLOCK), jnp.float32),
+            pltpu.SMEM((4,), jnp.int32),
             dma((4,)),
-            dma((4,)),
+            dma((5,)),
             dma((2, 4)),
             dma((4, 4)),
             dma((4,)),
-            dma((5, 4)),
-            dma((5, 4)),
+            dma((8, 4)),
+            dma((7, 4)),
             dma((3,)),
             dma((3,)),
             dma((3,)),
             dma((3,)),
         ],
         compiler_params=pltpu.CompilerParams(
-            collective_id=0, has_side_effects=True, vmem_limit_bytes=48 * 1024 * 1024
+            collective_id=0, has_side_effects=True, vmem_limit_bytes=60 * 1024 * 1024
         ),
         name="screen",
     )(features, clusters.reshape(-1, 128), bands)

time: 133 us -> 88.1 us (0.66)
  the two profiles are of different devices: /device:TPU:2 before, /device:TPU:65 now
where the time goes in v2:
time: 88.1 us; the launch traced here: 87.9 us
  Pallas kernels  85.4 us (97%)
  local copies, waits for them, and re-layouts  1.86 us (2%)
    pallas_call x1, Pallas kernels, on_device(): pl.pallas_call(functools.partial(kernel, runs), out_shape=[jax.ShapeDtype...  85.4 us
    unnamed x6, local copies, waits for them, and re-layouts  1.86 us

profile of v2, /device:TPU:65, one launch (start us, length us, event | category | flops | bytes accessed | tf_op | source)
XLA Modules:
  0.0 87.9 jit_solution(17039029769083595169)
XLA Ops:
  0.6 85.4 %screen.1 = (f32[1,256]{1,0:T(1,128)}, f32[1,256]{1,0:T(1,128)}) custom-call(bf16[1024,512]{1,0:T(8,128)(2,1)} %features.1, s32[1024,128]{1,0:T(8,128)} %bitcast.3, s32[4]{0:T(128)} %bands_in.1), custom_call_target="tpu_custom_call" | custom-call | tf_op jit(solution)/shard_map/screen/pallas_call | solution.py:586
  86.0 0.0 copy-start.1
  86.0 0.7 copy-done.1
  86.7 0.0 copy-start
  86.7 0.6 copy.7
  87.2 0.1 copy-done
  87.3 0.6 copy.8
Async XLA Ops:
  86.0 0.7 copy-start.1
  86.7 0.6 copy-start

commit v3 on v2

--- a/solution.py
+++ b/solution.py
@@ -201,7 +201,7 @@
         def _():
             send_below(3, own, r, PASS1, None)
 
-        @pl.when(drops & first_ring & near)
+        @pl.when(drops & first_ring & (near if r > 1 else True))
         def _():
             send_below(3, own, r, PASS1, FIRST)
 
@@ -210,7 +210,7 @@
 
         @pl.when(drops & first_ring & near)
         def _():
-            if piece in (1, 3):
+            if piece == 1:
                 arrived(piece, 2)
             run, slot = (shifted(-layer), VIA1) if r in Z_FIRST else (below, PASS1)
             ahead_copy(7, whole.at[piece, 2], r, run, slot, mate(2)).start()
@@ -366,17 +366,13 @@
             relay_layer(3)
 
         relay_pass(3)
-        relay_rest(2)
-        send_other(2)
         relay_soon(1, FIRST)
-        relay_rest(3)
-        send_other(3)
+
+        @pl.when(far)
+        def _():
+            relay_layer(0)
+
         relay_pass(2)
-
-        @pl.when(far)
-        def _():
-            relay_layer(0)
-
         relay_cross(0, FIRST)
         relay_cross(1, FIRST)
         for r in (3, 2):
@@ -385,6 +381,8 @@
         for r in ORDER:
             relay_later(r)
         relay_layer_late(0)
+        relay_rest(2)
+        relay_rest(3)
         relay_layer_late(3)
         for r in ORDER:
             relay_second(r)
@@ -395,28 +393,31 @@
         relay_soon(1, None)
         relay_cross(1, None)
         relay_pass(coming[1])
-        relay_rest(2)
         relay_soon(3, None)
         relay_cross(3, None)
-        relay_rest(3)
+        relay_pass(coming[2])
+        relay_later(coming[0])
         relay_soon(2, None)
         relay_cross(2, None)
-        relay_pass(coming[2])
-        relay_later(coming[0])
         relay_pass(coming[3])
-        for r in coming[1:]:
-            relay_later(r)
-        for r in coming:
-            relay_last(r)
-
+        relay_later(coming[1])
+        relay_last(coming[0])
+        relay_later(coming[2])
+        relay_last(coming[1])
+        relay_later(coming[3])
+        relay_rest(2)
+        relay_rest(3)
+        relay_last(coming[2])
+        relay_last(coming[3])
+
+    for j in (1, 2, 3):
+        arrived(3, j)
     for j in (1, 3):
         arrived(1, j)
-        arrived(3, j)
 
     @pl.when(~(drops & first_ring & near))
     def _():
         arrived(1, 2)
-        arrived(3, 2)
 
     for i in range(5):
         label_loads[i].wait()
@@ -522,7 +523,11 @@
         key_stats, query_stats = tile(i, keys, inverse_norm(keys))
         key_msg[i - 1, 0:1, :] = key_stats[0]
         key_msg[i - 1, 1:2, :] = key_stats[1]
-        key_copy(i).start()
+
+        @pl.when(p + i < runs)
+        def _():
+            key_copy(i).start()
+
         if running is None:
             running = query_stats
         else:
@@ -545,13 +550,14 @@
         def _():
             sent(1, r)
 
-        @pl.when((drops & ~(first_ring & far)) | (odd & (column == 3)))
+        @pl.when((drops & (~(first_ring & far) if r > 1 else True)) | (odd & (column == 3)))
         def _():
             sent(3, r)
 
-        @pl.when(drops & first_ring & near)
-        def _():
-            sent(7, r)
+        if r > 1:
+            @pl.when(drops & first_ring & near)
+            def _():
+                sent(7, r)
 
         @pl.when(even & (((column == 0) & ~first_ring) | ((column == 2) & last_ring)))
         def _():
@@ -568,7 +574,19 @@
     to_chip(1).wait_send()
     to_chip(0).wait_send()
     for i in (1, 3, 2):
-        key_copy(i).wait()
+        @pl.when(p + i < runs)
+        def _():
+            key_copy(i).wait_send()
+
+        @pl.when(p >= i)
+        def _():
+            key_copy(i).wait_recv()
+
+        @pl.when(p < i)
+        def _():
+            key_got[i - 1, 0:1, :] = jnp.full((1, BLOCK), MASKED, jnp.float32)
+            key_got[i - 1, 1:2, :] = jnp.zeros((1, BLOCK), jnp.float32)
+
         state = merge(state, (key_got[i - 1, 0:1, :], key_got[i - 1, 1:2, :]))
     for j in (1, 2, 3):
         query_copy(j).wait()

time: 88.1 us -> 74.2 us (0.84)
  the two profiles are of different devices: /device:TPU:65 before, /device:TPU:129 now
where the time goes in v3:
time: 74.2 us; the launch traced here: 74.1 us
  Pallas kernels  71.6 us (96%)
  local copies, waits for them, and re-layouts  1.86 us (3%)
    pallas_call x1, Pallas kernels, on_device(): pl.pallas_call(functools.partial(kernel, runs), out_shape=[jax.ShapeDtype...  71.6 us
    unnamed x6, local copies, waits for them, and re-layouts  1.86 us

profile of v3, /device:TPU:129, one launch (start us, length us, event | category | flops | bytes accessed | tf_op | source)
XLA Modules:
  0.0 74.1 jit_solution(794095740113562373)
XLA Ops:
  0.6 71.6 %screen.1 = (f32[1,256]{1,0:T(1,128)}, f32[1,256]{1,0:T(1,128)}) custom-call(bf16[1024,512]{1,0:T(8,128)(2,1)} %features.1, s32[1024,128]{1,0:T(8,128)} %bitcast.3, s32[4]{0:T(128)} %bands_in.1), custom_call_target="tpu_custom_call" | custom-call | tf_op jit(solution)/shard_map/screen/pallas_call | solution.py:604
  72.2 0.0 copy-start.1
  72.2 0.7 copy-done.1
  72.9 0.0 copy-start
  72.9 0.6 copy.7
  73.4 0.1 copy-done
  73.5 0.6 copy.8
Async XLA Ops:
  72.2 0.7 copy-start.1
  72.9 0.6 copy-start

commit v4 on v3

--- a/solution.py
+++ b/solution.py
@@ -294,6 +294,13 @@
         arrived(2, piece)
         pass_on(piece).start()
 
+    def inverse_norm(blocks):
+        squares = [jnp.square(b.astype(jnp.float32)) for b in blocks]
+        return lax.rsqrt(
+            jnp.sum(squares[0] + squares[1] + squares[2] + squares[3], axis=1, keepdims=True)
+            + EPSILON
+        )
+
     to_core(1).start()
     to_chip(3).start()
     to_chip(2).start()
@@ -338,6 +345,11 @@
     to_chip(2).wait_send()
     to_chip(1).start()
     to_chip(0).start()
+    early_norms = []
+    arrived(1, 1)
+    arrived(3, 1)
+    for j in range(2):
+        early_norms.append(inverse_norm([whole[r, j] for r in range(4)]))
 
     @pl.when(~first_ring & ~last_ring)
     def _():
@@ -410,10 +422,9 @@
         relay_last(coming[2])
         relay_last(coming[3])
 
-    for j in (1, 2, 3):
+    for j in (2, 3):
         arrived(3, j)
-    for j in (1, 3):
-        arrived(1, j)
+    arrived(1, 3)
 
     @pl.when(~(drops & first_ring & near))
     def _():
@@ -421,13 +432,6 @@
 
     for i in range(5):
         label_loads[i].wait()
-
-    def inverse_norm(blocks):
-        squares = [jnp.square(b.astype(jnp.float32)) for b in blocks]
-        return lax.rsqrt(
-            jnp.sum(squares[0] + squares[1] + squares[2] + squares[3], axis=1, keepdims=True)
-            + EPSILON
-        )
 
     def label_row(i, block):
         return jnp.concatenate(
@@ -437,7 +441,7 @@
     query_inv, query_label = [], []
     own_inv = None
     for j in range(4):
-        inv = inverse_norm([whole[r, j] for r in range(4)])
+        inv = early_norms[j] if j < 2 else inverse_norm([whole[r, j] for r in range(4)])
         own_inv = inv if j == 0 else own_inv
         query_inv.append(as_row(inv))
         query_label.append(label_row(0, mate(j)))

time: 74.2 us -> 79.3 us (1.069)
  the two profiles are of different devices: /device:TPU:129 before, /device:TPU:62 now
where the time goes in v4:
time: 79.3 us; the launch traced here: 79.1 us
  Pallas kernels  76.6 us (97%)
  local copies, waits for them, and re-layouts  1.86 us (2%)
    pallas_call x1, Pallas kernels, on_device(): pl.pallas_call(functools.partial(kernel, runs), out_shape=[jax.ShapeDtype...  76.6 us
    unnamed x6, local copies, waits for them, and re-layouts  1.86 us

profile of v4, /device:TPU:62, one launch (start us, length us, event | category | flops | bytes accessed | tf_op | source)
XLA Modules:
  0.0 79.1 jit_solution(8689919951500838409)
XLA Ops:
  0.6 76.6 %screen.1 = (f32[1,256]{1,0:T(1,128)}, f32[1,256]{1,0:T(1,128)}) custom-call(bf16[1024,512]{1,0:T(8,128)(2,1)} %features.1, s32[1024,128]{1,0:T(8,128)} %bitcast.3, s32[4]{0:T(128)} %bands_in.1), custom_call_target="tpu_custom_call" | custom-call | tf_op jit(solution)/shard_map/screen/pallas_call | solution.py:608
  77.3 0.0 copy-start.1
  77.3 0.7 copy-done.1
  77.9 0.0 copy-start
  77.9 0.6 copy.7
  78.5 0.1 copy-done
  78.6 0.6 copy.8
Async XLA Ops:
  77.3 0.7 copy-start.1
  77.9 0.6 copy-start
